TPU v7x, 32 devices: a whole 2x2x4 slice. The times are simulated.
32 devices in a mesh: ctx: 8 (over y, x, core), exp: 4 (over z).
Axes of the slice: x: 2, y: 2, z: 4, core: 2. Of those that a mesh axis runs over, the one named last changes fastest.
Arguments:
- span_q: bfloat16 [1024, 6144], P('ctx', 'exp'), may hold values from -9 to 9
- prompt_kv: bfloat16 [2, 8192, 1024], P(None, 'ctx', 'exp'), may hold values from -10 to 10
- span_kv: bfloat16 [2, 1024, 1024], P(None, 'ctx', 'exp'), may hold values from -10 to 10
- decode_q: bfloat16 [128, 6144], P('ctx', 'exp'), may hold values from -4 to 4
- decode_cache: bfloat16 [2, 128, 256, 1024], P(None, 'ctx', None, 'exp'), may hold values from -10 to 10
- decode_new: bfloat16 [2, 128, 1024], P(None, 'ctx', 'exp'), may hold values from -10.5 to 10.5
- decode_len: int32 [128], P('ctx'), may hold values from 1 to 256, as said below
- residual: bfloat16 [1152, 6144], P('ctx', 'exp'), may hold values from -1.5 to 1.5
- norm_gain: bfloat16 [6144], P('exp'), may hold values from 0.099609375 to 1.8984375
- router: bfloat16 [6144, 8], P('exp'), may hold values from -0.078125 to 0.078125
- expert_ids: int32 [1152, 2], P('ctx'), may hold values from 0 to 7, all different within a row; in each aligned block of 144 rows (0 to 143, 144 to 287, ...) at most 40 rows name the same one
- capacity: int32 [8], replicated, may hold values from 20 to 40, as said below
- w_gate: bfloat16 [8, 6144, 8192], P('exp', None, 'ctx'), may hold values from -0.078125 to 0.078125
- w_up: bfloat16 [8, 6144, 8192], P('exp', None, 'ctx'), may hold values from -0.078125 to 0.078125
- w_down: bfloat16 [8, 8192, 6144], P('exp', 'ctx'), may hold values from -0.0625 to 0.0625
Outputs:
- mixed: bfloat16 [1152, 6144], P('ctx', 'exp')
Inputs may be any that keep to these rules, and one draw needn't show every extreme that they name: `decode_len`: some decode row has exactly 256 cached positions. Some expert's capacity is exactly 40. `expert_ids`: in each row block of 144 rows (the rows of one ctx index) no expert is named by more than 40 rows; in some block some expert is named by exactly 40 rows.
All inputs are finite; a program needn't handle non-finite values.
Results may differ from a plain program's by a relative error of at most 0.019.
Values may be sent and summed in bfloat16 or wider, within the bound.
A program may use at most 192 MiB of HBM per device.

v0:
```python
import jax
import jax.numpy as jnp
from jax import lax
from jax.sharding import PartitionSpec as P

D = 6144
HD = 128
QPK = 6
EXPERTS = 8
TOPK = 2
CAP = 40


NEG = -1e30
EPS = 1e-05


def from_behind(value, axis, steps):
    count = lax.axis_size(axis)
    pairs = [(source, (source + steps) % count) for source in range(count)]
    return lax.ppermute(value, axis, pairs)


def fold_block(state, queries, keys, values, visible):
    best, total, summed = state
    scores = jnp.einsum(
        "cgqd,kgd->gqck", queries, keys, preferred_element_type=jnp.float32
    ) * HD ** (-0.5)
    shown = visible[None, None, :, :]
    scores = jnp.where(shown, scores, NEG)
    newest = jnp.maximum(best, jnp.max(scores, axis=-1))
    factor = jnp.exp(best - newest)
    weights = jnp.where(shown, jnp.exp(scores - newest[..., None]), 0.0)
    total = total * factor + jnp.sum(weights, axis=-1)
    summed = summed * factor[..., None] + jnp.einsum(
        "gqck,kgd->gqcd", weights.astype(jnp.bfloat16), values, preferred_element_type=jnp.float32
    )
    return (newest, total, summed)


def decode_block(decode_q, decode_cache, decode_new, decode_len, groups):
    rows = decode_q.shape[0]
    length = decode_cache.shape[2]
    queries = decode_q.reshape(rows, groups, QPK, HD)
    keys = decode_cache[0].reshape(rows, length, groups, HD)
    values = decode_cache[1].reshape(rows, length, groups, HD)
    own_key = decode_new[0].reshape(rows, groups, HD)
    own_value = decode_new[1].reshape(rows, groups, HD)
    scale = HD ** (-0.5)
    scores = (
        jnp.einsum("rgqd,rlgd->rgql", queries, keys, preferred_element_type=jnp.float32) * scale
    )
    live = (jnp.arange(length, dtype=jnp.int32)[None, :] < decode_len[:, None])[:, None, None, :]
    own = jnp.einsum("rgqd,rgd->rgq", queries, own_key, preferred_element_type=jnp.float32) * scale
    top = jnp.maximum(jnp.max(jnp.where(live, scores, NEG), axis=-1), own)
    weights = jnp.where(live, jnp.exp(scores - top[..., None]), 0.0)
    own_weight = jnp.exp(own - top)
    own_prob = lax.optimization_barrier(own_weight.astype(jnp.bfloat16)).astype(jnp.float32)
    summed = jnp.einsum(
        "rgql,rlgd->rgqd", weights.astype(jnp.bfloat16), values, preferred_element_type=jnp.float32
    )
    summed = summed + own_prob[..., None] * own_value.astype(jnp.float32)[:, :, None, :]
    result = summed / (jnp.sum(weights, axis=-1) + own_weight)[..., None]
    return result.reshape(rows, groups * QPK * HD).astype(jnp.bfloat16)


def on_device(
    span_q,
    prompt_kv,
    span_kv,
    decode_q,
    decode_cache,
    decode_new,
    decode_len,
    residual,
    norm_gain,
    router,
    expert_ids,
    capacity,
    w_gate,
    w_up,
    w_down,
):
    groups = prompt_kv.shape[2] // HD
    span_rows = span_q.shape[0]
    prompt_rows = prompt_kv.shape[1]
    local_width = prompt_rows + span_rows
    loop_size = lax.axis_size("ctx")
    here = lax.axis_index("ctx")
    queries = span_q.reshape(span_rows, groups, QPK, HD)
    local_kv = jnp.concatenate([prompt_kv, span_kv], axis=1)
    keys = local_kv[0].reshape(local_width, groups, HD)
    values = local_kv[1].reshape(local_width, groups, HD)
    query_place = jnp.arange(span_rows, dtype=jnp.int32)
    key_place = jnp.arange(local_width, dtype=jnp.int32)
    empty = (
        jnp.full((groups, QPK, span_rows), NEG, jnp.float32),
        jnp.zeros((groups, QPK, span_rows), jnp.float32),
        jnp.zeros((groups, QPK, span_rows, HD), jnp.float32),
    )

    def visible_from(source):
        span_key = here * span_rows + key_place - prompt_rows
        span_query = source * span_rows + query_place
        return (key_place[None, :] < prompt_rows) | (span_key[None, :] <= span_query[:, None])

    def loop_step(step, carry):
        moving, best, total, summed = carry
        source = (here - step) % loop_size
        best, total, summed = fold_block(
            (best, total, summed), moving, keys, values, visible_from(source)
        )
        moving = from_behind(moving, "ctx", 1)
        best, total, summed = from_behind((best, total, summed), "ctx", 1)
        return (moving, best, total, summed)

    leftover, best, total, summed = lax.fori_loop(0, loop_size, loop_step, (queries,) + empty)
    span_out = (
        (summed / total[..., None])
        .transpose(2, 0, 1, 3)
        .reshape(span_rows, groups * QPK * HD)
        .astype(jnp.bfloat16)
    )
    decode_out = decode_block(decode_q, decode_cache, decode_new, decode_len, groups)
    attn = jnp.concatenate([span_out, decode_out], axis=0)
    carried = residual.astype(jnp.float32) + attn.astype(jnp.float32)
    gained = carried * norm_gain.astype(jnp.float32)
    squares = jnp.sum(carried * carried, axis=1)
    partial_logits = jnp.dot(gained, router.astype(jnp.float32), precision=lax.Precision.HIGHEST)
    squares, logits = lax.psum((squares, partial_logits), "exp")
    rscale = lax.rsqrt(squares / D + EPS)
    logits = logits * rscale[:, None]
    normed = (gained * rscale[:, None]).astype(jnp.bfloat16)
    row_count = expert_ids.shape[0]
    slots = CAP * EXPERTS
    expert_range = jnp.arange(EXPERTS, dtype=jnp.int32)
    onehot = expert_ids[:, :, None] == expert_range[None, None, :]
    chosen = jnp.sum(jnp.where(onehot, logits[:, None, :], 0.0), axis=-1)
    route_weight = jax.nn.sigmoid(chosen - chosen[:, ::-1])
    flat_ids = expert_ids.reshape(row_count * TOPK)
    assign = onehot.reshape(row_count * TOPK, EXPERTS).astype(jnp.int32)
    prior = jnp.cumsum(assign, axis=0) - assign
    position = jnp.sum(prior * assign, axis=1)
    limit = jnp.sum(assign * capacity[None, :], axis=1)
    kept = position < limit
    slot_index = position * EXPERTS + flat_ids
    select = kept[:, None] & (slot_index[:, None] == jnp.arange(slots, dtype=jnp.int32)[None, :])
    select = select.reshape(row_count, TOPK, slots)
    placing = jnp.sum(select.astype(jnp.float32), axis=1).astype(jnp.bfloat16)
    outgoing = jnp.einsum("rs,rd->sd", placing, normed, preferred_element_type=jnp.float32).astype(
        jnp.bfloat16
    )
    outgoing = outgoing.reshape(CAP, EXPERTS, normed.shape[1])
    arrived = lax.all_to_all(outgoing, "exp", split_axis=1, concat_axis=2, tiled=True)
    piece = lax.all_gather(arrived, "ctx", axis=0, tiled=True)
    gate = jnp.einsum("red,edf->ref", piece, w_gate, preferred_element_type=jnp.float32)
    up = jnp.einsum("red,edf->ref", piece, w_up, preferred_element_type=jnp.float32)
    hidden = (jax.nn.silu(gate) * up).astype(jnp.bfloat16)
    result = lax.psum_scatter(
        jnp.einsum("ref,efd->red", hidden, w_down, preferred_element_type=jnp.float32).astype(
            jnp.bfloat16
        ),
        "ctx",
        scatter_dimension=0,
        tiled=True,
    )
    returned = lax.all_to_all(result, "exp", split_axis=2, concat_axis=1, tiled=True)
    returned = returned.reshape(slots, returned.shape[2]).astype(jnp.float32)
    mixing = jnp.sum(select.astype(jnp.float32) * route_weight[:, :, None], axis=1)
    moe = jnp.dot(mixing, returned, precision=lax.Precision.HIGHEST)
    return (carried + moe).astype(jnp.bfloat16)


def solution(mesh):
    placed = (
        P("ctx", "exp"),
        P(None, "ctx", "exp"),
        P(None, "ctx", "exp"),
        P("ctx", "exp"),
        P(None, "ctx", None, "exp"),
        P(None, "ctx", "exp"),
        P("ctx"),
        P("ctx", "exp"),
        P("exp"),
        P("exp", None),
        P("ctx", None),
        P(),
        P("exp", None, "ctx"),
        P("exp", None, "ctx"),
        P("exp", "ctx", None),
    )
    return jax.shard_map(
        on_device, mesh=mesh, in_specs=placed, out_specs=P("ctx", "exp"), check_vma=False
    )
```

profile of v0, /device:TPU:9, one launch (start us, length us, event | category | flops | bytes accessed | tf_op | source)
XLA Modules:
  0.0 500.7 jit_solution(15145541689703806354)
XLA Ops:
  18.5 184.0 %while.23 = (s32[]{:T(128)}, bf16[128,2,6,128]{3,0,2,1:T(8,128)(2,1)S(1)}, f32[2,6,128]{2,1,0:T(8,128)S(1)}, f32[2,6,128]{2,1,0:T(8,128)S(1)}, f32[2,6,128,128]{...) while((s32[]{:T(128)}, ...), condition=%wide.region_3.4_spmd.clone.clone, body=%wide.region_0.3_spmd.clone.clone.sunk | while | flops 929667584 | bytes 30622384 | solution.py:117
  29.1 11.8 %collective-permute-done.1 = f32[2,6,128]{2,1,0:T(8,128)S(1)} collective-permute-done((f32[2,6,128]{2,1,0:T(8,128)S(1)}, f32[2,6,128]{2,1,0:T(8,128)S(1)}, u32[]{:S(2)}, u32[]{:S(2)}) %collective-permute-start.1) | collective-permute-done | bytes 6176 | tf_op jit(solution)/shard_map/while/body/eval_jaxpr/ppermute | solution.py:21
  53.1 10.9 %collective-permute-done.1 = f32[2,6,128]{2,1,0:T(8,128)S(1)} collective-permute-done((f32[2,6,128]{2,1,0:T(8,128)S(1)}, f32[2,6,128]{2,1,0:T(8,128)S(1)}, u32[]{:S(2)}, u32[]{:S(2)}) %collective-permute-start.1) | collective-permute-done | bytes 6176 | tf_op jit(solution)/shard_map/while/body/eval_jaxpr/ppermute | solution.py:21
  77.1 10.0 %collective-permute-done.1 = f32[2,6,128]{2,1,0:T(8,128)S(1)} collective-permute-done((f32[2,6,128]{2,1,0:T(8,128)S(1)}, f32[2,6,128]{2,1,0:T(8,128)S(1)}, u32[]{:S(2)}, u32[]{:S(2)}) %collective-permute-start.1) | collective-permute-done | bytes 6176 | tf_op jit(solution)/shard_map/while/body/eval_jaxpr/ppermute | solution.py:21
  101.0 9.1 %collective-permute-done.1 = f32[2,6,128]{2,1,0:T(8,128)S(1)} collective-permute-done((f32[2,6,128]{2,1,0:T(8,128)S(1)}, f32[2,6,128]{2,1,0:T(8,128)S(1)}, u32[]{:S(2)}, u32[]{:S(2)}) %collective-permute-start.1) | collective-permute-done | bytes 6176 | tf_op jit(solution)/shard_map/while/body/eval_jaxpr/ppermute | solution.py:21
  125.0 8.2 %collective-permute-done.1 = f32[2,6,128]{2,1,0:T(8,128)S(1)} collective-permute-done((f32[2,6,128]{2,1,0:T(8,128)S(1)}, f32[2,6,128]{2,1,0:T(8,128)S(1)}, u32[]{:S(2)}, u32[]{:S(2)}) %collective-permute-start.1) | collective-permute-done | bytes 6176 | tf_op jit(solution)/shard_map/while/body/eval_jaxpr/ppermute | solution.py:21
  149.0 7.3 %collective-permute-done.1 = f32[2,6,128]{2,1,0:T(8,128)S(1)} collective-permute-done((f32[2,6,128]{2,1,0:T(8,128)S(1)}, f32[2,6,128]{2,1,0:T(8,128)S(1)}, u32[]{:S(2)}, u32[]{:S(2)}) %collective-permute-start.1) | collective-permute-done | bytes 6176 | tf_op jit(solution)/shard_map/while/body/eval_jaxpr/ppermute | solution.py:21
  173.0 6.4 %collective-permute-done.1 = f32[2,6,128]{2,1,0:T(8,128)S(1)} collective-permute-done((f32[2,6,128]{2,1,0:T(8,128)S(1)}, f32[2,6,128]{2,1,0:T(8,128)S(1)}, u32[]{:S(2)}, u32[]{:S(2)}) %collective-permute-start.1) | collective-permute-done | bytes 6176 | tf_op jit(solution)/shard_map/while/body/eval_jaxpr/ppermute | solution.py:21
  189.1 4.5 collective-permute-start
  197.0 5.5 %collective-permute-done.1 = f32[2,6,128]{2,1,0:T(8,128)S(1)} collective-permute-done((f32[2,6,128]{2,1,0:T(8,128)S(1)}, f32[2,6,128]{2,1,0:T(8,128)S(1)}, u32[]{:S(2)}, u32[]{:S(2)}) %collective-permute-start.1) | collective-permute-done | bytes 6176 | tf_op jit(solution)/shard_map/while/body/eval_jaxpr/ppermute | solution.py:21
  203.2 4.7 fusion.48
  216.2 7.2 %all-reduce.1 = (f32[144,8]{0,1:T(8,128)S(1)}, f32[144]{0:T(256)S(1)}) all-reduce(f32[144,8]{0,1:T(8,128)S(1)} %fusion.29, f32[144]{0:T(256)S(1)} %multiply_reduce_fusion), channel_id=1, replica_groups=mesh['ctx'=8,'exp'=4] {'exp'}, use_global_device_ids=true, to_apply=%region_10.11 | all-reduce | flops 1296 | bytes 10368 | tf_op jit(solution)/shard_map/psum | solution.py:130
  224.6 18.6 %all_to_all.33 = bf16[40,8,1536]{2,0,1:T(8,128)(2,1)S(1)} all-to-all(bf16[40,8,1536]{2,0,1:T(8,128)(2,1)S(1)} %copy.99), channel_id=1, replica_groups=mesh['ctx'=8,'exp'=4] {'exp'}, dimensions={1} | all-to-all | bytes 1966080 | tf_op jit(solution)/shard_map/all_to_all | solution.py:154
  245.9 66.6 %all-gather.2.cloned.1.call-done = bf16[320,2,6144]{2,0,1:T(8,128)(2,1)} async-done(((bf16[40,2,6144]{2,0,1:T(8,128)(2,1)}), bf16[320,2,6144]{2,0,1:T(8,128)(2,1)}) %all-gather.2.cloned.1.call-update) | async-done | bytes 7864336 | tf_op jit(solution)/shard_map/all_gather | solution.py:155
  312.5 15.3 %fusion.50 = f32[2,320,1024]{2,1,0:T(8,128)S(1)} fusion(bf16[320,2,6144]{2,0,1:T(8,128)(2,1)} %all-gather.2.cloned.1.call-done, bf16[2,6144,1024]{2,1,0:T(8,128)(2,1)} %param.29), kind=kOutput, calls=%fused_computation.91 | convolution fusion | flops 8053063680 | bytes 35651584 | tf_op jit(solution)/shard_map/red,edf->ref/dot_general | solution.py:156
  327.8 16.8 %fusion.21 = bf16[320,2,1024]{2,0,1:T(8,128)(2,1)} fusion(f32[2,320,1024]{2,1,0:T(8,128)S(1)} %fusion.50, bf16[320,2,6144]{2,0,1:T(8,128)(2,1)} %all-gather.2.cloned.1.call-done, bf16[2,6144,1024]{2,1,0:T(8,128)(2,1)} %param.30), kind=kOutput, calls=%fused_computation.27 | convolution fusion | flops 8056995840 | bytes 36962304 | tf_op jit(solution)/shard_map/red,edf->ref/dot_general | solution.py:157
  344.5 16.9 %fusion.20 = bf16[2,40,8,6144]{3,2,1,0:T(8,128)(2,1)S(1)} fusion(bf16[320,2,1024]{2,0,1:T(8,128)(2,1)} %fusion.21, bf16[2,1024,6144]{2,1,0:T(8,128)(2,1)} %param.31), kind=kOutput, calls=%fused_computation.24 | convolution fusion | flops 8056995840 | bytes 34340864 | tf_op jit(solution)/shard_map/ref,efd->red/dot_general | solution.py:160
  365.1 69.1 %reduce-scatter.4.cloned.1.call-done = bf16[40,12288]{1,0:T(8,128)(2,1)} async-done(((bf16[320,12288]{1,0:T(8,128)(2,1)}), bf16[40,12288]{1,0:T(8,128)(2,1)}) %reduce-scatter.4.cloned.1.call-update) | async-done | bytes 983056
  434.2 3.7 reshape.186
  437.9 7.1 %copy.101 = bf16[40,2,6144]{0,1,2:T(2,128)(2,1)S(1)} copy(bf16[40,2,6144]{2,1,0:T(2,128)(2,1)} %reshape.186) | data formatting | bytes 1966080 | tf_op jit(solution)/shard_map/reduce_scatter | solution.py:159
  445.1 5.9 %reshape.188 = bf16[4,2,61440]{2,1,0:T(2,128)(2,1)} reshape(bf16[6144,2,40]{2,1,0:T(2,128)(2,1)S(1)} %bitcast.105) | data formatting | bytes 1966080
  451.0 26.7 %all_to_all.34 = bf16[4,2,61440]{2,1,0:T(2,128)(2,1)} all-to-all(bf16[4,2,61440]{2,1,0:T(2,128)(2,1)} %reshape.188), channel_id=1, replica_groups=mesh['ctx'=8,'exp'=4] {'exp'}, dimensions={0} | all-to-all | bytes 1966080 | tf_op jit(solution)/shard_map/all_to_all | solution.py:167
  477.7 5.7 %reshape.189 = bf16[6144,2,40]{2,1,0:T(2,128)(2,1)S(1)} reshape(bf16[4,2,61440]{2,1,0:T(2,128)(2,1)} %all_to_all.34) | data formatting | bytes 1966080
  483.4 5.2 %copy.102 = bf16[40,2,4,1536]{3,1,2,0:T(2,128)(2,1)} copy(bf16[40,2,4,1536]{0,1,3,2:T(2,128)(2,1)S(1)} %bitcast.106) | data formatting | bytes 1966080 | tf_op jit(solution)/shard_map/all_to_all | solution.py:167
  (209 shorter events, 143.1 us)
Async XLA Ops:
  6.5 305.9 %all-gather.2.cloned.1.call-start = ((), (), s32[]{:S(2)}) async-start(), calls=%async_computation.3 | async-start | bytes 8847360 | tf_op jit(solution)/shard_map/all_gather | solution.py:155
  25.6 15.3 %collective-permute-start.3 = (f32[2,6,128,128]{3,2,1,0:T(8,128)}, f32[2,6,128,128]{3,2,1,0:T(8,128)S(1)}, u32[]{:S(2)}, u32[]{:S(2)}) collective-permute-start(f32[2,6,128,128]{3,2,1,0:T(8,128)} %fusion.80), channel_id=1, source_target_pairs={{0,4},{4,8},{8,12},{12,16},{16,20},{20,24},{24,28},{28,0},{1,5},{5... | collective-permute-start | bytes 2359304 | tf_op jit(solution)/shard_map/while/body/eval_jaxpr/ppermute | solution.py:21
  27.4 13.5 %collective-permute-start = (bf16[128,2,6,128]{3,0,2,1:T(8,128)(2,1)S(1)}, bf16[128,2,6,128]{3,0,2,1:T(8,128)(2,1)S(1)}, u32[]{:S(2)}, u32[]{:S(2)}) collective-permute-start(bf16[128,2,6,128]{3,0,2,1:T(8,128)(2,1)S(1)} %copy.124), channel_id=1, source_target_pairs={{0,4},{4,8},{8,12},{12,16},{16,20},{20,24},{24,28},{28,0},{1,5},{5... | collective-permute-start | bytes 1179656 | tf_op jit(solution)/shard_map/while/body/eval_jaxpr/ppermute | solution.py:21
  27.5 13.4 %collective-permute-start.1 = (f32[2,6,128]{2,1,0:T(8,128)S(1)}, f32[2,6,128]{2,1,0:T(8,128)S(1)}, u32[]{:S(2)}, u32[]{:S(2)}) collective-permute-start(f32[2,6,128]{2,1,0:T(8,128)S(1)} %max.22), channel_id=1, source_target_pairs={{0,4},{4,8},{8,12},{12,16},{16,20},{20,24},{24,28},{28,0},{1,5},{5... | collective-permute-start | bytes 18440 | tf_op jit(solution)/shard_map/while/body/eval_jaxpr/ppermute | solution.py:21
  29.0 11.9 %collective-permute-start.2 = (f32[2,6,128]{2,1,0:T(8,128)S(1)}, f32[2,6,128]{2,1,0:T(8,128)S(1)}, u32[]{:S(2)}, u32[]{:S(2)}) collective-permute-start(f32[2,6,128]{2,1,0:T(8,128)S(1)} %get-tuple-element.443), channel_id=1, source_target_pairs={{0,4},{4,8},{8,12},{12,16},{16,20},{20,24},{24,28},{28,0},{1,5},{5... | collective-permute-start | bytes 18440 | tf_op jit(solution)/shard_map/while/body/eval_jaxpr/ppermute | solution.py:21
  48.0 16.0 %collective-permute-start.3 = (f32[2,6,128,128]{3,2,1,0:T(8,128)}, f32[2,6,128,128]{3,2,1,0:T(8,128)S(1)}, u32[]{:S(2)}, u32[]{:S(2)}) collective-permute-start(f32[2,6,128,128]{3,2,1,0:T(8,128)} %fusion.80), channel_id=1, source_target_pairs={{0,4},{4,8},{8,12},{12,16},{16,20},{20,24},{24,28},{28,0},{1,5},{5... | collective-permute-start | bytes 2359304 | tf_op jit(solution)/shard_map/while/body/eval_jaxpr/ppermute | solution.py:21
  50.5 13.5 %collective-permute-start = (bf16[128,2,6,128]{3,0,2,1:T(8,128)(2,1)S(1)}, bf16[128,2,6,128]{3,0,2,1:T(8,128)(2,1)S(1)}, u32[]{:S(2)}, u32[]{:S(2)}) collective-permute-start(bf16[128,2,6,128]{3,0,2,1:T(8,128)(2,1)S(1)} %copy.124), channel_id=1, source_target_pairs={{0,4},{4,8},{8,12},{12,16},{16,20},{20,24},{24,28},{28,0},{1,5},{5... | collective-permute-start | bytes 1179656 | tf_op jit(solution)/shard_map/while/body/eval_jaxpr/ppermute | solution.py:21
  50.5 13.4 %collective-permute-start.1 = (f32[2,6,128]{2,1,0:T(8,128)S(1)}, f32[2,6,128]{2,1,0:T(8,128)S(1)}, u32[]{:S(2)}, u32[]{:S(2)}) collective-permute-start(f32[2,6,128]{2,1,0:T(8,128)S(1)} %max.22), channel_id=1, source_target_pairs={{0,4},{4,8},{8,12},{12,16},{16,20},{20,24},{24,28},{28,0},{1,5},{5... | collective-permute-start | bytes 18440 | tf_op jit(solution)/shard_map/while/body/eval_jaxpr/ppermute | solution.py:21
  71.1 16.0 %collective-permute-start.3 = (f32[2,6,128,128]{3,2,1,0:T(8,128)}, f32[2,6,128,128]{3,2,1,0:T(8,128)S(1)}, u32[]{:S(2)}, u32[]{:S(2)}) collective-permute-start(f32[2,6,128,128]{3,2,1,0:T(8,128)} %fusion.80), channel_id=1, source_target_pairs={{0,4},{4,8},{8,12},{12,16},{16,20},{20,24},{24,28},{28,0},{1,5},{5... | collective-permute-start | bytes 2359304 | tf_op jit(solution)/shard_map/while/body/eval_jaxpr/ppermute | solution.py:21
  73.6 13.5 %collective-permute-start = (bf16[128,2,6,128]{3,0,2,1:T(8,128)(2,1)S(1)}, bf16[128,2,6,128]{3,0,2,1:T(8,128)(2,1)S(1)}, u32[]{:S(2)}, u32[]{:S(2)}) collective-permute-start(bf16[128,2,6,128]{3,0,2,1:T(8,128)(2,1)S(1)} %copy.124), channel_id=1, source_target_pairs={{0,4},{4,8},{8,12},{12,16},{16,20},{20,24},{24,28},{28,0},{1,5},{5... | collective-permute-start | bytes 1179656 | tf_op jit(solution)/shard_map/while/body/eval_jaxpr/ppermute | solution.py:21
  73.6 13.4 %collective-permute-start.1 = (f32[2,6,128]{2,1,0:T(8,128)S(1)}, f32[2,6,128]{2,1,0:T(8,128)S(1)}, u32[]{:S(2)}, u32[]{:S(2)}) collective-permute-start(f32[2,6,128]{2,1,0:T(8,128)S(1)} %max.22), channel_id=1, source_target_pairs={{0,4},{4,8},{8,12},{12,16},{16,20},{20,24},{24,28},{28,0},{1,5},{5... | collective-permute-start | bytes 18440 | tf_op jit(solution)/shard_map/while/body/eval_jaxpr/ppermute | solution.py:21
  94.2 16.0 %collective-permute-start.3 = (f32[2,6,128,128]{3,2,1,0:T(8,128)}, f32[2,6,128,128]{3,2,1,0:T(8,128)S(1)}, u32[]{:S(2)}, u32[]{:S(2)}) collective-permute-start(f32[2,6,128,128]{3,2,1,0:T(8,128)} %fusion.80), channel_id=1, source_target_pairs={{0,4},{4,8},{8,12},{12,16},{16,20},{20,24},{24,28},{28,0},{1,5},{5... | collective-permute-start | bytes 2359304 | tf_op jit(solution)/shard_map/while/body/eval_jaxpr/ppermute | solution.py:21
  96.7 13.5 %collective-permute-start = (bf16[128,2,6,128]{3,0,2,1:T(8,128)(2,1)S(1)}, bf16[128,2,6,128]{3,0,2,1:T(8,128)(2,1)S(1)}, u32[]{:S(2)}, u32[]{:S(2)}) collective-permute-start(bf16[128,2,6,128]{3,0,2,1:T(8,128)(2,1)S(1)} %copy.124), channel_id=1, source_target_pairs={{0,4},{4,8},{8,12},{12,16},{16,20},{20,24},{24,28},{28,0},{1,5},{5... | collective-permute-start | bytes 1179656 | tf_op jit(solution)/shard_map/while/body/eval_jaxpr/ppermute | solution.py:21
  97.6 12.5 %collective-permute-start.1 = (f32[2,6,128]{2,1,0:T(8,128)S(1)}, f32[2,6,128]{2,1,0:T(8,128)S(1)}, u32[]{:S(2)}, u32[]{:S(2)}) collective-permute-start(f32[2,6,128]{2,1,0:T(8,128)S(1)} %max.22), channel_id=1, source_target_pairs={{0,4},{4,8},{8,12},{12,16},{16,20},{20,24},{24,28},{28,0},{1,5},{5... | collective-permute-start | bytes 18440 | tf_op jit(solution)/shard_map/while/body/eval_jaxpr/ppermute | solution.py:21
  117.3 16.0 %collective-permute-start.3 = (f32[2,6,128,128]{3,2,1,0:T(8,128)}, f32[2,6,128,128]{3,2,1,0:T(8,128)S(1)}, u32[]{:S(2)}, u32[]{:S(2)}) collective-permute-start(f32[2,6,128,128]{3,2,1,0:T(8,128)} %fusion.80), channel_id=1, source_target_pairs={{0,4},{4,8},{8,12},{12,16},{16,20},{20,24},{24,28},{28,0},{1,5},{5... | collective-permute-start | bytes 2359304 | tf_op jit(solution)/shard_map/while/body/eval_jaxpr/ppermute | solution.py:21
  119.8 13.5 %collective-permute-start = (bf16[128,2,6,128]{3,0,2,1:T(8,128)(2,1)S(1)}, bf16[128,2,6,128]{3,0,2,1:T(8,128)(2,1)S(1)}, u32[]{:S(2)}, u32[]{:S(2)}) collective-permute-start(bf16[128,2,6,128]{3,0,2,1:T(8,128)(2,1)S(1)} %copy.124), channel_id=1, source_target_pairs={{0,4},{4,8},{8,12},{12,16},{16,20},{20,24},{24,28},{28,0},{1,5},{5... | collective-permute-start | bytes 1179656 | tf_op jit(solution)/shard_map/while/body/eval_jaxpr/ppermute | solution.py:21
  121.6 11.6 %collective-permute-start.1 = (f32[2,6,128]{2,1,0:T(8,128)S(1)}, f32[2,6,128]{2,1,0:T(8,128)S(1)}, u32[]{:S(2)}, u32[]{:S(2)}) collective-permute-start(f32[2,6,128]{2,1,0:T(8,128)S(1)} %max.22), channel_id=1, source_target_pairs={{0,4},{4,8},{8,12},{12,16},{16,20},{20,24},{24,28},{28,0},{1,5},{5... | collective-permute-start | bytes 18440 | tf_op jit(solution)/shard_map/while/body/eval_jaxpr/ppermute | solution.py:21
  140.4 16.0 %collective-permute-start.3 = (f32[2,6,128,128]{3,2,1,0:T(8,128)}, f32[2,6,128,128]{3,2,1,0:T(8,128)S(1)}, u32[]{:S(2)}, u32[]{:S(2)}) collective-permute-start(f32[2,6,128,128]{3,2,1,0:T(8,128)} %fusion.80), channel_id=1, source_target_pairs={{0,4},{4,8},{8,12},{12,16},{16,20},{20,24},{24,28},{28,0},{1,5},{5... | collective-permute-start | bytes 2359304 | tf_op jit(solution)/shard_map/while/body/eval_jaxpr/ppermute | solution.py:21
  142.9 13.5 %collective-permute-start = (bf16[128,2,6,128]{3,0,2,1:T(8,128)(2,1)S(1)}, bf16[128,2,6,128]{3,0,2,1:T(8,128)(2,1)S(1)}, u32[]{:S(2)}, u32[]{:S(2)}) collective-permute-start(bf16[128,2,6,128]{3,0,2,1:T(8,128)(2,1)S(1)} %copy.124), channel_id=1, source_target_pairs={{0,4},{4,8},{8,12},{12,16},{16,20},{20,24},{24,28},{28,0},{1,5},{5... | collective-permute-start | bytes 1179656 | tf_op jit(solution)/shard_map/while/body/eval_jaxpr/ppermute | solution.py:21
  163.5 16.0 %collective-permute-start.3 = (f32[2,6,128,128]{3,2,1,0:T(8,128)}, f32[2,6,128,128]{3,2,1,0:T(8,128)S(1)}, u32[]{:S(2)}, u32[]{:S(2)}) collective-permute-start(f32[2,6,128,128]{3,2,1,0:T(8,128)} %fusion.80), channel_id=1, source_target_pairs={{0,4},{4,8},{8,12},{12,16},{16,20},{20,24},{24,28},{28,0},{1,5},{5... | collective-permute-start | bytes 2359304 | tf_op jit(solution)/shard_map/while/body/eval_jaxpr/ppermute | solution.py:21
  166.0 13.5 %collective-permute-start = (bf16[128,2,6,128]{3,0,2,1:T(8,128)(2,1)S(1)}, bf16[128,2,6,128]{3,0,2,1:T(8,128)(2,1)S(1)}, u32[]{:S(2)}, u32[]{:S(2)}) collective-permute-start(bf16[128,2,6,128]{3,0,2,1:T(8,128)(2,1)S(1)} %copy.124), channel_id=1, source_target_pairs={{0,4},{4,8},{8,12},{12,16},{16,20},{20,24},{24,28},{28,0},{1,5},{5... | collective-permute-start | bytes 1179656 | tf_op jit(solution)/shard_map/while/body/eval_jaxpr/ppermute | solution.py:21
  186.6 16.0 %collective-permute-start.3 = (f32[2,6,128,128]{3,2,1,0:T(8,128)}, f32[2,6,128,128]{3,2,1,0:T(8,128)S(1)}, u32[]{:S(2)}, u32[]{:S(2)}) collective-permute-start(f32[2,6,128,128]{3,2,1,0:T(8,128)} %fusion.80), channel_id=1, source_target_pairs={{0,4},{4,8},{8,12},{12,16},{16,20},{20,24},{24,28},{28,0},{1,5},{5... | collective-permute-start | bytes 2359304 | tf_op jit(solution)/shard_map/while/body/eval_jaxpr/ppermute | solution.py:21
  189.1 13.5 %collective-permute-start = (bf16[128,2,6,128]{3,0,2,1:T(8,128)(2,1)S(1)}, bf16[128,2,6,128]{3,0,2,1:T(8,128)(2,1)S(1)}, u32[]{:S(2)}, u32[]{:S(2)}) collective-permute-start(bf16[128,2,6,128]{3,0,2,1:T(8,128)(2,1)S(1)} %copy.124), channel_id=1, source_target_pairs={{0,4},{4,8},{8,12},{12,16},{16,20},{20,24},{24,28},{28,0},{1,5},{5... | collective-permute-start | bytes 1179656 | tf_op jit(solution)/shard_map/while/body/eval_jaxpr/ppermute | solution.py:21
  245.8 188.4 %reduce-scatter.4.cloned.1.call-start = ((), (), s32[]{:S(2)}) async-start(), calls=%async_computation.4 | async-start | bytes 8847360
  (15 other events, 386.6 us)
Sparse Core Ops, SparseCore 0:
  246.0 66.4 all-gather.1
  365.2 68.9 reduce-scatter.3
where the time goes:
time: 506 us; the launch traced here: 501 us
  waiting for transfers between devices  206 us (41%)
  matrix products  89.1 us (18%)
  starting transfers between devices  57.6 us (11%)
  local copies, waits for them, and re-layouts  55.1 us (11%)
  blocking collectives  52.6 us (10%)
  other arithmetic  26.3 us (5%)
  between operations  13.8 us (3%)
    ppermute x32, waiting for transfers between devices, from_behind(): return lax.ppermute(value, axis, pairs)  69.9 us
    unnamed x3, waiting for transfers between devices  69.2 us
    all_gather x1, waiting for transfers between devices, on_device(): piece = lax.all_gather(arrived, 'ctx', axis=0, tiled=True)  66.6 us
    ppermute x32, starting transfers between devices, from_behind(): return lax.ppermute(value, axis, pairs)  57.5 us
    unnamed x23, local copies, waits for them, and re-layouts  30 us
    all_to_all x1, blocking collectives, on_device(): lax.all_to_all(result, 'exp', split_axis=2, concat_axis=1, tiled=True)  26.7 us
    dot_general x8, matrix products, fold_block(): jnp.einsum('gqck,kgd->gqcd', weights.astype(jnp.bfloat16), values, prefer...  25.9 us
    all_to_all x1, blocking collectives, on_device(): lax.all_to_all(outgoing, 'exp', split_axis=1, concat_axis=2, tiled=True)  18.6 us
  transfers between devices with their start and end apart: 34, of which 18 were waited for; matrix products, arithmetic and copies ran while one was open for 0% of the time, Pallas kernels for 0%

commit v1 on v0

--- a/solution.py
+++ b/solution.py
@@ -1,6 +1,10 @@
+import functools
+
 import jax
 import jax.numpy as jnp
 from jax import lax
+from jax.experimental import pallas as pl
+from jax.experimental.pallas import tpu as pltpu
 from jax.sharding import PartitionSpec as P
 
 D = 6144
@@ -62,6 +66,282 @@
     summed = summed + own_prob[..., None] * own_value.astype(jnp.float32)[:, :, None, :]
     result = summed / (jnp.sum(weights, axis=-1) + own_weight)[..., None]
     return result.reshape(rows, groups * QPK * HD).astype(jnp.bfloat16)
+
+
+def greet(axis, count, me):
+    barrier = pltpu.get_barrier_semaphore()
+    for step in range(1, count):
+        pl.semaphore_signal(
+            barrier,
+            inc=1,
+            device_id={axis: lax.rem(me + step, count)},
+            device_id_type=pl.DeviceIdType.MESH,
+        )
+    pl.semaphore_wait(barrier, count - 1)
+
+
+def remote(source, target, send, recv, axis, device):
+    return pltpu.make_async_remote_copy(
+        src_ref=source,
+        dst_ref=target,
+        send_sem=send,
+        recv_sem=recv,
+        device_id={axis: device},
+        device_id_type=pl.DeviceIdType.MESH,
+    )
+
+
+def exchange_kernel(axis, count, blocks, paired, *refs):
+    total = len(blocks) + paired
+    ins, outs = refs[:total], refs[total : 2 * total]
+    send, recv, local = refs[2 * total :]
+    me = lax.axis_index(axis)
+    greet(axis, count, me)
+    copies = []
+    for k in range(len(blocks), total):
+        parity = lax.rem(me, 2)
+        copies.append(
+            remote(
+                ins[k].at[1 - parity], outs[k], send.at[0, k], recv.at[0, k], axis, me + 1 - 2 * parity
+            )
+        )
+    for step in range(1, count):
+        to = lax.rem(me + step, count)
+        for k, amount in enumerate(blocks):
+            copies.append(
+                remote(
+                    ins[k].at[lax.rem(to, amount)],
+                    outs[k].at[me],
+                    send.at[step, k],
+                    recv.at[step, k],
+                    axis,
+                    to,
+                )
+            )
+    for copy in copies:
+        copy.start()
+    own = []
+    for k, amount in enumerate(blocks):
+        own.append(
+            pltpu.make_async_copy(ins[k].at[lax.rem(me, amount)], outs[k].at[me], local.at[k])
+        )
+        own[-1].start()
+    for copy in own:
+        copy.wait()
+    for copy in copies:
+        copy.wait()
+
+
+def exchange(axis, arrays, pairs, collective_id):
+    count = lax.axis_size(axis)
+    blocks = tuple(a.shape[0] for a in arrays)
+    total = len(arrays) + len(pairs)
+    shapes = [jax.ShapeDtypeStruct((count,) + a.shape[1:], a.dtype) for a in arrays]
+    shapes += [jax.ShapeDtypeStruct(a.shape[1:], a.dtype) for a in pairs]
+    return pl.pallas_call(
+        functools.partial(exchange_kernel, axis, count, blocks, len(pairs)),
+        out_shape=shapes,
+        in_specs=[pl.BlockSpec(memory_space=pl.ANY)] * total,
+        out_specs=[pl.BlockSpec(memory_space=pl.ANY)] * total,
+        scratch_shapes=[
+            pltpu.SemaphoreType.DMA((count, total)),
+            pltpu.SemaphoreType.DMA((count, total)),
+            pltpu.SemaphoreType.DMA((total,)),
+        ],
+        compiler_params=pltpu.CompilerParams(collective_id=collective_id, has_side_effects=True),
+    )(*arrays, *pairs)
+
+
+def gather_kernel(x, out, send, recv, local):
+    me = lax.axis_index("ctx")
+    core = lax.rem(me, 2)
+    column = lax.rem(me // 2, 2)
+    line = me // 4
+    buddy = me + 1 - 2 * core
+    side = me + 2 - 4 * column
+    across = me + 4 - 8 * line
+    corner = side + across - me
+    greet("ctx", 8, me)
+
+    def relay(k, source, target, device):
+        return remote(source, target, send.at[k], recv.at[k], "ctx", device)
+
+    def arrival(k, target):
+        return relay(k, target, target, buddy)
+
+    near = [
+        relay(0, x, out.at[me], side),
+        relay(1, x, out.at[me], across),
+        relay(2, x, out.at[me], buddy),
+    ]
+    for copy in near:
+        copy.start()
+    own = pltpu.make_async_copy(x, out.at[me], local)
+    own.start()
+    arrival(0, out.at[side]).wait_recv()
+    far = [
+        relay(3, out.at[side, 0], out.at[side, 0], across),
+        relay(4, out.at[side], out.at[side], buddy),
+    ]
+    for copy in far:
+        copy.start()
+    arrival(1, out.at[across]).wait_recv()
+    more = [
+        relay(5, out.at[across, 1], out.at[across, 1], side),
+        relay(6, out.at[across], out.at[across], buddy),
+    ]
+    for copy in more:
+        copy.start()
+    arrival(3, out.at[corner, 0]).wait_recv()
+    last = [relay(7, out.at[corner, 0], out.at[corner, 0], buddy)]
+    last[0].start()
+    arrival(5, out.at[corner, 1]).wait_recv()
+    last.append(relay(8, out.at[corner, 1], out.at[corner, 1], buddy))
+    last[1].start()
+    arrival(2, out.at[buddy]).wait_recv()
+    arrival(4, out.at[buddy + side - me]).wait_recv()
+    arrival(6, out.at[buddy + across - me]).wait_recv()
+    arrival(7, out.at[buddy + corner - me, 0]).wait_recv()
+    arrival(8, out.at[buddy + corner - me, 1]).wait_recv()
+    for copy in near + far + more + last:
+        copy.wait_send()
+    own.wait()
+
+
+def gather(x, collective_id):
+    return pl.pallas_call(
+        gather_kernel,
+        out_shape=jax.ShapeDtypeStruct((8,) + x.shape, x.dtype),
+        in_specs=[pl.BlockSpec(memory_space=pl.ANY)],
+        out_specs=pl.BlockSpec(memory_space=pl.ANY),
+        scratch_shapes=[
+            pltpu.SemaphoreType.DMA((9,)),
+            pltpu.SemaphoreType.DMA((9,)),
+            pltpu.SemaphoreType.DMA,
+        ],
+        compiler_params=pltpu.CompilerParams(collective_id=collective_id, has_side_effects=True),
+    )(x)
+
+
+def part_kernel(rows, tile, q_ref, k_ref, v_ref, place_ref, out_ref, lse_ref):
+    source = pl.program_id(0)
+    span = place_ref.shape[1]
+    plain = k_ref.shape[0] - span
+    place = source * rows + lax.broadcasted_iota(jnp.int32, (tile, span), 0) % rows
+    shown = place_ref[...] <= place
+    for start in range(0, q_ref.shape[1], tile):
+        scores = lax.dot_general(
+            q_ref[0, start : start + tile, :],
+            k_ref[...],
+            (((1,), (1,)), ((), ())),
+            preferred_element_type=jnp.float32,
+        ) * HD ** (-0.5)
+        scores = jnp.concatenate(
+            [scores[:, :plain], jnp.where(shown, scores[:, plain:], NEG)], axis=1
+        )
+        top = jnp.max(scores, axis=1, keepdims=True)
+        probs = jnp.exp(scores - top).astype(jnp.bfloat16)
+        summed = jnp.dot(probs, v_ref[...], preferred_element_type=jnp.float32)
+        total = summed[:, HD:]
+        out_ref[0, start : start + tile, :] = (summed[:, :HD] / total).astype(jnp.bfloat16)
+        lse = (top + jnp.log(total)).T
+        lse_ref[0, :, start : start + tile] = lse[:8, :]
+
+
+def span_parts(queries, keys, values, place, rows):
+    count, stacked, _ = queries.shape
+    width = keys.shape[0]
+    tile = 2 * rows
+    return pl.pallas_call(
+        functools.partial(part_kernel, rows, tile),
+        grid=(count,),
+        out_shape=[
+            jax.ShapeDtypeStruct((count, stacked, HD), jnp.bfloat16),
+            jax.ShapeDtypeStruct((count, 8, stacked), jnp.float32),
+        ],
+        in_specs=[
+            pl.BlockSpec((1, stacked, HD), lambda i: (i, 0, 0)),
+            pl.BlockSpec((width, HD), lambda i: (0, 0)),
+            pl.BlockSpec((width, 2 * HD), lambda i: (0, 0)),
+            pl.BlockSpec((1, place.shape[1]), lambda i: (0, 0)),
+        ],
+        out_specs=[
+            pl.BlockSpec((1, stacked, HD), lambda i: (i, 0, 0)),
+            pl.BlockSpec((1, 8, stacked), lambda i: (i, 0, 0)),
+        ],
+        compiler_params=pltpu.CompilerParams(vmem_limit_bytes=48 * 1024 * 1024),
+    )(queries, keys, values, place)
+
+
+def split_span(span_q, prompt_kv, span_kv):
+    rows = span_q.shape[0]
+    prompt_rows = prompt_kv.shape[1]
+    here = lax.axis_index("ctx")
+    core = here % 2
+    buddy = here + 1 - 2 * core
+    by_group = span_q.reshape(rows, 2, QPK, HD).transpose(1, 2, 0, 3).reshape(2, QPK * rows, HD)
+    local_kv = jnp.concatenate([prompt_kv, span_kv], axis=1)
+    kv = local_kv.reshape(2, prompt_rows + rows, 2, HD).transpose(2, 0, 1, 3)
+    queries, other = exchange("ctx", [by_group], [kv], 0)
+    own = jnp.where(core == 0, kv[0], kv[1])
+    joined = jnp.concatenate(
+        [own[:, :prompt_rows], other[:, :prompt_rows], own[:, prompt_rows:], other[:, prompt_rows:]],
+        axis=1,
+    )
+    spots = jnp.arange(rows, dtype=jnp.int32)
+    place = jnp.concatenate([here * rows + spots, buddy * rows + spots])[None, :]
+    values = jnp.concatenate([joined[1], jnp.ones_like(joined[1])], axis=1)
+    parts, lse = span_parts(queries, joined[0], values, place, rows)
+    parts, lse = exchange("ctx", [parts, lse], [], 1)
+    lse = lse[:, 0].reshape(-1, 2, QPK, rows)
+    weight = jnp.exp(lse - jnp.max(lse, axis=0, keepdims=True))
+    weight = weight / jnp.sum(weight, axis=0, keepdims=True)
+    parts = parts.reshape(-1, 2, QPK, rows, HD).astype(jnp.float32)
+    result = jnp.sum(weight[..., None] * parts, axis=0)
+    return result.transpose(2, 0, 1, 3).reshape(rows, 2 * QPK * HD).astype(jnp.bfloat16)
+
+
+def ring_span(span_q, prompt_kv, span_kv):
+    groups = prompt_kv.shape[2] // HD
+    span_rows = span_q.shape[0]
+    prompt_rows = prompt_kv.shape[1]
+    local_width = prompt_rows + span_rows
+    loop_size = lax.axis_size("ctx")
+    here = lax.axis_index("ctx")
+    queries = span_q.reshape(span_rows, groups, QPK, HD)
+    local_kv = jnp.concatenate([prompt_kv, span_kv], axis=1)
+    keys = local_kv[0].reshape(local_width, groups, HD)
+    values = local_kv[1].reshape(local_width, groups, HD)
+    query_place = jnp.arange(span_rows, dtype=jnp.int32)
+    key_place = jnp.arange(local_width, dtype=jnp.int32)
+    empty = (
+        jnp.full((groups, QPK, span_rows), NEG, jnp.float32),
+        jnp.zeros((groups, QPK, span_rows), jnp.float32),
+        jnp.zeros((groups, QPK, span_rows, HD), jnp.float32),
+    )
+
+    def visible_from(source):
+        span_key = here * span_rows + key_place - prompt_rows
+        span_query = source * span_rows + query_place
+        return (key_place[None, :] < prompt_rows) | (span_key[None, :] <= span_query[:, None])
+
+    def loop_step(step, carry):
+        moving, best, total, summed = carry
+        source = (here - step) % loop_size
+        best, total, summed = fold_block(
+            (best, total, summed), moving, keys, values, visible_from(source)
+        )
+        moving = from_behind(moving, "ctx", 1)
+        best, total, summed = from_behind((best, total, summed), "ctx", 1)
+        return (moving, best, total, summed)
+
+    leftover, best, total, summed = lax.fori_loop(0, loop_size, loop_step, (queries,) + empty)
+    return (
+        (summed / total[..., None])
+        .transpose(2, 0, 1, 3)
+        .reshape(span_rows, groups * QPK * HD)
+        .astype(jnp.bfloat16)
+    )
 
 
 def on_device(
@@ -82,52 +362,23 @@
     w_down,
 ):
     groups = prompt_kv.shape[2] // HD
-    span_rows = span_q.shape[0]
-    prompt_rows = prompt_kv.shape[1]
-    local_width = prompt_rows + span_rows
-    loop_size = lax.axis_size("ctx")
-    here = lax.axis_index("ctx")
-    queries = span_q.reshape(span_rows, groups, QPK, HD)
-    local_kv = jnp.concatenate([prompt_kv, span_kv], axis=1)
-    keys = local_kv[0].reshape(local_width, groups, HD)
-    values = local_kv[1].reshape(local_width, groups, HD)
-    query_place = jnp.arange(span_rows, dtype=jnp.int32)
-    key_place = jnp.arange(local_width, dtype=jnp.int32)
-    empty = (
-        jnp.full((groups, QPK, span_rows), NEG, jnp.float32),
-        jnp.zeros((groups, QPK, span_rows), jnp.float32),
-        jnp.zeros((groups, QPK, span_rows, HD), jnp.float32),
-    )
-
-    def visible_from(source):
-        span_key = here * span_rows + key_place - prompt_rows
-        span_query = source * span_rows + query_place
-        return (key_place[None, :] < prompt_rows) | (span_key[None, :] <= span_query[:, None])
-
-    def loop_step(step, carry):
-        moving, best, total, summed = carry
-        source = (here - step) % loop_size
-        best, total, summed = fold_block(
-            (best, total, summed), moving, keys, values, visible_from(source)
-        )
-        moving = from_behind(moving, "ctx", 1)
-        best, total, summed = from_behind((best, total, summed), "ctx", 1)
-        return (moving, best, total, summed)
-
-    leftover, best, total, summed = lax.fori_loop(0, loop_size, loop_step, (queries,) + empty)
-    span_out = (
-        (summed / total[..., None])
-        .transpose(2, 0, 1, 3)
-        .reshape(span_rows, groups * QPK * HD)
-        .astype(jnp.bfloat16)
-    )
+    paired = lax.axis_size("ctx") == 8 and groups == 2
+    spread = split_span if paired else ring_span
+    span_out = spread(span_q, prompt_kv, span_kv)
     decode_out = decode_block(decode_q, decode_cache, decode_new, decode_len, groups)
     attn = jnp.concatenate([span_out, decode_out], axis=0)
     carried = residual.astype(jnp.float32) + attn.astype(jnp.float32)
     gained = carried * norm_gain.astype(jnp.float32)
     squares = jnp.sum(carried * carried, axis=1)
     partial_logits = jnp.dot(gained, router.astype(jnp.float32), precision=lax.Precision.HIGHEST)
-    squares, logits = lax.psum((squares, partial_logits), "exp")
+    if paired:
+        sums = jnp.concatenate([partial_logits, squares[:, None]], axis=1).T
+        sums = jnp.pad(sums, ((0, 16 - sums.shape[0]), (0, -sums.shape[1] % 128)))
+        (sums,) = exchange("exp", [sums[None]], [], 2)
+        sums = jnp.sum(sums, axis=0)[:, : squares.shape[0]].T
+        squares, logits = sums[:, EXPERTS], sums[:, :EXPERTS]
+    else:
+        squares, logits = lax.psum((squares, partial_logits), "exp")
     rscale = lax.rsqrt(squares / D + EPS)
     logits = logits * rscale[:, None]
     normed = (gained * rscale[:, None]).astype(jnp.bfloat16)
@@ -143,29 +394,41 @@
     position = jnp.sum(prior * assign, axis=1)
     limit = jnp.sum(assign * capacity[None, :], axis=1)
     kept = position < limit
-    slot_index = position * EXPERTS + flat_ids
+    slot_index = flat_ids * CAP + position
     select = kept[:, None] & (slot_index[:, None] == jnp.arange(slots, dtype=jnp.int32)[None, :])
     select = select.reshape(row_count, TOPK, slots)
     placing = jnp.sum(select.astype(jnp.float32), axis=1).astype(jnp.bfloat16)
     outgoing = jnp.einsum("rs,rd->sd", placing, normed, preferred_element_type=jnp.float32).astype(
         jnp.bfloat16
     )
-    outgoing = outgoing.reshape(CAP, EXPERTS, normed.shape[1])
-    arrived = lax.all_to_all(outgoing, "exp", split_axis=1, concat_axis=2, tiled=True)
-    piece = lax.all_gather(arrived, "ctx", axis=0, tiled=True)
-    gate = jnp.einsum("red,edf->ref", piece, w_gate, preferred_element_type=jnp.float32)
-    up = jnp.einsum("red,edf->ref", piece, w_up, preferred_element_type=jnp.float32)
+    features = normed.shape[1]
+    owners = lax.axis_size("exp")
+    held = EXPERTS // owners
+    outgoing = outgoing.reshape(owners, held, CAP, features)
+    if paired:
+        (arrived,) = exchange("exp", [outgoing], [], 3)
+        arrived = arrived.transpose(1, 2, 0, 3).reshape(held, CAP, owners * features)
+        piece = gather(arrived, 4)
+    else:
+        arrived = lax.all_to_all(outgoing, "exp", split_axis=0, concat_axis=3, tiled=True)[0]
+        piece = lax.all_gather(arrived, "ctx", axis=0)
+    gate = jnp.einsum("necd,edf->encf", piece, w_gate, preferred_element_type=jnp.float32)
+    up = jnp.einsum("necd,edf->encf", piece, w_up, preferred_element_type=jnp.float32)
     hidden = (jax.nn.silu(gate) * up).astype(jnp.bfloat16)
     result = lax.psum_scatter(
-        jnp.einsum("ref,efd->red", hidden, w_down, preferred_element_type=jnp.float32).astype(
+        jnp.einsum("encf,efd->necd", hidden, w_down, preferred_element_type=jnp.float32).astype(
             jnp.bfloat16
         ),
         "ctx",
         scatter_dimension=0,
         tiled=True,
-    )
-    returned = lax.all_to_all(result, "exp", split_axis=2, concat_axis=1, tiled=True)
-    returned = returned.reshape(slots, returned.shape[2]).astype(jnp.float32)
+    )[0]
+    if paired:
+        result = result.reshape(held, CAP, owners, features).transpose(2, 0, 1, 3)
+        (returned,) = exchange("exp", [result], [], 5)
+    else:
+        returned = lax.all_to_all(result[None], "exp", split_axis=3, concat_axis=0, tiled=True)
+    returned = returned.reshape(slots, features).astype(jnp.float32)
     mixing = jnp.sum(select.astype(jnp.float32) * route_weight[:, :, None], axis=1)
     moe = jnp.dot(mixing, returned, precision=lax.Precision.HIGHEST)
     return (carried + moe).astype(jnp.bfloat16)

time: 506 us -> 395 us (0.78)
  Pallas kernels: 0 us -> 167 us
  waiting for transfers between devices: 206 us -> 119 us
  starting transfers between devices: 57.6 us -> 0.01 us
  blocking collectives: 52.6 us -> 0 us
  matrix products: 89.1 us -> 59.2 us
  local copies, waits for them, and re-layouts: 55.1 us -> 30.2 us
  other arithmetic: 26.3 us -> 5.29 us
    pallas_call x0 -> x7, Pallas kernels: none -> 167 us  [the longest x5 101 us: exchange(): pl.pallas_call(functools.partial(exchange_kernel, axis, count, blocks, le...]
    ppermute x32 -> x0, waiting for transfers between devices: 69.9 us -> none  [from_behind(): return lax.ppermute(value, axis, pairs)]
    all_gather x1 -> x0, waiting for transfers between devices: 66.6 us -> none  [on_device(): piece = lax.all_gather(arrived, 'ctx', axis=0, tiled=True)]
    ppermute x32 -> x0, starting transfers between devices: 57.5 us -> none  [from_behind(): return lax.ppermute(value, axis, pairs)]
    unnamed x3 -> x2, waiting for transfers between devices: 69.2 us -> 119 us
    all_to_all x2 -> x0, blocking collectives: 45.4 us -> none  [the longest x1 26.7 us: on_device(): lax.all_to_all(result, 'exp', split_axis=2, concat_axis=1, tiled=True)]
    dot_general x19 -> x3, matrix products: 83.9 us -> 51.4 us  [the longest x1 18.6 us: on_device(): jnp.einsum('encf,efd->necd', hidden, w_down, preferred_element_type=jnp.f...]
    unnamed x23 -> x40, local copies, waits for them, and re-layouts: 30 us -> 14.4 us
  transfers between devices with their start and end apart: 34 -> 1, of which waited for: 18 -> 1; matrix products, arithmetic and copies ran while one was open for 0% -> 0% of each run, Pallas kernels for 0% -> 0%
where the time goes in v1:
time: 395 us; the launch traced here: 394 us
  Pallas kernels  167 us (42%)
  waiting for transfers between devices  119 us (30%)
  matrix products  59.2 us (15%)
  local copies, waits for them, and re-layouts  30.2 us (8%)
  between operations  13.9 us (4%)
  other arithmetic  5.29 us (1%)
    unnamed x2, waiting for transfers between devices  119 us
    pallas_call x5, Pallas kernels, exchange(): pl.pallas_call(functools.partial(exchange_kernel, axis, count, blocks, le...  101 us
    pallas_call x1, Pallas kernels, gather(): pl.pallas_call(gather_kernel, out_shape=jax.ShapeDtypeStruct((8,) + x.sha...  40.3 us
    pallas_call x1, Pallas kernels, span_parts(): pl.pallas_call(functools.partial(part_kernel, rows, tile), grid=(count,),...  25.8 us
    dot_general x1, matrix products, on_device(): jnp.einsum('encf,efd->necd', hidden, w_down, preferred_element_type=jnp.f...  18.6 us
    dot_general x1, matrix products, on_device(): jnp.einsum('necd,edf->encf', piece, w_gate, preferred_element_type=jnp.fl...  16.7 us
    dot_general x1, matrix products, on_device(): jnp.einsum('necd,edf->encf', piece, w_up, preferred_element_type=jnp.floa...  16.1 us
    unnamed x40, local copies, waits for them, and re-layouts  14.4 us
  transfers between devices with their start and end apart: 1, of which 1 were waited for; matrix products, arithmetic and copies ran while one was open for 0% of the time, Pallas kernels for 0%

profile of v1, /device:TPU:9, one launch (start us, length us, event | category | flops | bytes accessed | tf_op | source)
XLA Modules:
  0.0 394.5 jit_solution(11122796714117807107)
XLA Ops:
  6.5 1.3 copy.80
  10.5 1.4 copy.84
  11.9 21.5 %shard_map.145 = (bf16[8,768,128]{2,1,0:T(8,128)(2,1)}, bf16[2,1152,128]{2,1,0:T(8,128)(2,1)}) custom-call(bf16[2,768,128]{2,1,0:T(8,128)(2,1)} %bitcast.99, bf16[2,2,1152,128]{3,2,1,0:T(8,128)(2,1)} %bitcast.87), custom_call_target="tpu_custom_call" | custom-call | tf_op jit(solution)/shard_map/pallas_call | solution.py:141
  37.5 3.9 %fusion.45 = (bf16[1,16,256,256]{3,2,1,0:T(8,128)(2,1)}, bf16[1,16,256,256]{3,2,1,0:T(8,128)(2,1)S(1)}) fusion(bf16[2,16,256,256]{3,2,1,0:T(8,128)(2,1)} %param.19), kind=kLoop, calls=%fused_computation.84 | loop fusion | bytes 8388608 | tf_op jit(solution)/shard_map/slice | solution.py:49
  41.5 2.4 copy.108
  44.1 2.9 copy.107
  47.9 2.3 fusion.21
  50.7 1.2 copy-done.2
  51.8 25.8 %shard_map.146 = (bf16[8,768,128]{2,1,0:T(8,128)(2,1)S(1)}, f32[8,8,768]{2,1,0:T(8,128)S(1)}) custom-call(bf16[8,768,128]{2,1,0:T(8,128)(2,1)S(1)} %copy-done.2, bf16[2304,128]{1,0:T(8,128)(2,1)S(1)} %get-tuple-element.24.k_ref, bf16[2304,256]{1,0:T(8,128)(2,1)S(1)} %concatenate.20.v_ref, s32[1,256]{1,0:T(1,128)S(1)} %bitcast.86), custom_call_target="tpu_custom_call" | custom-call | tf_op jit(solution)/shard_map/pallas_call | solution.py:255
  77.7 1.2 copy-done.3
  79.5 22.9 %shard_map.147 = (bf16[8,768,128]{2,1,0:T(8,128)(2,1)}, f32[8,8,768]{2,1,0:T(8,128)}) custom-call(bf16[8,768,128]{2,1,0:T(8,128)(2,1)} %copy-done.3, f32[8,8,768]{2,1,0:T(8,128)} %copy-done.4), custom_call_target="tpu_custom_call" | custom-call | tf_op jit(solution)/shard_map/pallas_call | solution.py:141
  103.6 2.2 fusion.14
  107.8 5.5 %shard_map.148 = f32[4,16,256]{2,1,0:T(8,128)} custom-call(f32[1,16,256]{2,1,0:T(8,128)} %pad_bitcast_fusion.refs_0_), custom_call_target="tpu_custom_call" | custom-call | tf_op jit(solution)/shard_map/pallas_call | solution.py:141
  114.5 1.5 convolution_convert_fusion
  116.0 25.6 %shard_map.149 = bf16[4,2,40,1536]{3,2,1,0:T(8,128)(2,1)} custom-call(bf16[4,2,40,1536]{3,2,1,0:T(8,128)(2,1)} %bitcast.101), custom_call_target="tpu_custom_call" | custom-call | tf_op jit(solution)/shard_map/pallas_call | solution.py:141
  141.6 2.3 copy.109
  143.9 40.3 %shard_map.150 = bf16[8,2,40,6144]{3,2,1,0:T(8,128)(2,1)} custom-call(bf16[2,40,6144]{2,1,0:T(8,128)(2,1)} %bitcast.93), custom_call_target="tpu_custom_call" | custom-call | tf_op jit(solution)/shard_map/pallas_call | solution.py:212
  184.2 16.7 %fusion.4 = f32[2,8,40,1024]{3,2,1,0:T(8,128)} fusion(bf16[2,6144,1024]{2,1,0:T(8,128)(2,1)} %param.27, bf16[8,2,40,6144]{3,2,1,0:T(8,128)(2,1)} %shard_map.150), kind=kOutput, calls=%fused_computation.4 | convolution fusion | flops 8053063680 | bytes 35651584 | tf_op jit(solution)/shard_map/necd,edf->encf/dot_general | solution.py:415
  200.8 16.1 %multiply_convert_fusion = bf16[2,8,40,1024]{3,2,1,0:T(8,128)(2,1)S(1)} fusion(f32[2,8,40,1024]{3,2,1,0:T(8,128)} %fusion.4, bf16[2,6144,1024]{2,1,0:T(8,128)(2,1)} %param.28, bf16[8,2,40,6144]{3,2,1,0:T(8,128)(2,1)} %shard_map.150), kind=kOutput, calls=%fused_computation.13 | convolution fusion | flops 8056995840 | bytes 36962304 | tf_op jit(solution)/shard_map/necd,edf->encf/dot_general | solution.py:416
  217.0 18.6 %fusion.9 = bf16[8,2,40,6144]{3,2,0,1:T(8,128)(2,1)} fusion(bf16[2,8,40,1024]{3,2,1,0:T(8,128)(2,1)S(1)} %multiply_convert_fusion, bf16[2,1024,6144]{2,1,0:T(8,128)(2,1)} %param.29), kind=kOutput, calls=%fused_computation.7 | convolution fusion | flops 8056995840 | bytes 34340864 | tf_op jit(solution)/shard_map/encf,efd->necd/dot_general | solution.py:419
  236.8 119.1 %all-reduce.6.cloned.1.call-done = bf16[8,2,40,6144]{3,2,0,1:T(8,128)(2,1)} async-done(((bf16[8,2,40,6144]{3,2,0,1:T(8,128)(2,1)}), bf16[8,2,40,6144]{3,2,0,1:T(8,128)(2,1)}) %all-reduce.6.cloned.1.call-update) | async-done | bytes 7864336
  355.9 1.9 constant_dynamic-slice_fusion
  359.7 25.0 %shard_map.151 = bf16[4,2,40,1536]{3,2,1,0:T(8,128)(2,1)} custom-call(bf16[4,2,40,1536]{3,2,1,0:T(8,128)(2,1)} %bitcast.94), custom_call_target="tpu_custom_call" | custom-call | tf_op jit(solution)/shard_map/pallas_call | solution.py:141
  384.8 2.8 fusion.15
  (98 shorter events, 16.0 us)
Async XLA Ops:
  6.5 100.0 %copy-start = (bf16[1536,8]{0,1:T(8,128)(2,1)S(1)}, bf16[1536,8]{0,1:T(8,128)(2,1)}, u32[]{:S(2)}) copy-start(bf16[1536,8]{0,1:T(8,128)(2,1)} %param.24) | copy-start | bytes 73732
  6.5 3.3 copy-start.8
  6.5 349.4 %all-reduce.6.cloned.1.call-start = ((), (), s32[]{:S(2)}) async-start(), calls=%async_computation | async-start | bytes 15728640
  11.9 23.5 %copy-start.5 = (bf16[2,1152,2,128]{3,1,0,2:T(8,128)(2,1)S(1)}, bf16[2,1152,2,128]{3,1,0,2:T(8,128)(2,1)}, u32[]{:S(2)}) copy-start(bf16[2,1152,2,128]{3,1,0,2:T(8,128)(2,1)} %copy.84) | copy-start | bytes 3538948
  33.4 2.1 copy-start.10
  33.4 3.5 copy-start.13
  35.5 6.0 %copy-start.6 = (bf16[2,1152,128]{2,1,0:T(8,128)(2,1)}, bf16[2,1152,128]{2,1,0:T(8,128)(2,1)S(1)}, u32[]{:S(2)}) copy-start(bf16[2,1152,128]{2,1,0:T(8,128)(2,1)S(1)} %fusion.24) | copy-start | bytes 1769476
  41.5 2.4 copy-start.14
  41.5 2.5 copy-start.9
  43.9 3.0 copy-start.11
  47.6 2.7 slice-start
  47.6 2.7 slice-start.1
  50.4 1.4 copy-start.2
  77.7 1.2 copy-start.3
  78.8 0.7 copy-start.4
  102.4 3.8 copy-start.12
  102.5 3.8 copy-start.7
  235.6 0.7 copy-start.15
  358.6 29.0 %copy-start.1 = (bf16[1536,8]{0,1:T(8,128)(2,1)S(1)}, bf16[1536,8]{0,1:T(8,128)(2,1)}, u32[]{:S(2)}) copy-start(bf16[1536,8]{0,1:T(8,128)(2,1)} %param.24) | copy-start | bytes 73732
Sparse Core Ops, SparseCore 0:
  235.7 120.1 all-reduce.5

commit v2 on v1

--- a/solution.py
+++ b/solution.py
@@ -415,14 +415,9 @@
     gate = jnp.einsum("necd,edf->encf", piece, w_gate, preferred_element_type=jnp.float32)
     up = jnp.einsum("necd,edf->encf", piece, w_up, preferred_element_type=jnp.float32)
     hidden = (jax.nn.silu(gate) * up).astype(jnp.bfloat16)
-    result = lax.psum_scatter(
-        jnp.einsum("encf,efd->necd", hidden, w_down, preferred_element_type=jnp.float32).astype(
-            jnp.bfloat16
-        ),
-        "ctx",
-        scatter_dimension=0,
-        tiled=True,
-    )[0]
+    parts = jnp.einsum("encf,efd->nced", hidden, w_down, preferred_element_type=jnp.float32)
+    parts = parts.astype(jnp.bfloat16).reshape(-1, held, owners * features)
+    result = lax.psum_scatter(parts, "ctx", scatter_dimension=0, tiled=True).transpose(1, 0, 2)
     if paired:
         result = result.reshape(held, CAP, owners, features).transpose(2, 0, 1, 3)
         (returned,) = exchange("exp", [result], [], 5)

time: 395 us -> 343 us (0.87)
  waiting for transfers between devices: 119 us -> 68.4 us
    unnamed x2, waiting for transfers between devices: 119 us -> 68.4 us
    unnamed x40 -> x44, local copies, waits for them, and re-layouts: 14.4 us -> 16.8 us
where the time goes in v2:
time: 343 us; the launch traced here: 342 us
  Pallas kernels  166 us (48%)
  waiting for transfers between devices  68.4 us (20%)
  matrix products  55.5 us (16%)
  local copies, waits for them, and re-layouts  31.7 us (9%)
  between operations  13.9 us (4%)
  other arithmetic  5.98 us (2%)
    pallas_call x5, Pallas kernels, exchange(): pl.pallas_call(functools.partial(exchange_kernel, axis, count, blocks, le...  101 us
    unnamed x2, waiting for transfers between devices  68.4 us
    pallas_call x1, Pallas kernels, gather(): pl.pallas_call(gather_kernel, out_shape=jax.ShapeDtypeStruct((8,) + x.sha...  40.3 us
    pallas_call x1, Pallas kernels, span_parts(): pl.pallas_call(functools.partial(part_kernel, rows, tile), grid=(count,),...  25.5 us
    dot_general x1, matrix products, on_device(): jnp.einsum('encf,efd->nced', hidden, w_down, preferred_element_type=jnp.f...  17 us
    unnamed x44, local copies, waits for them, and re-layouts  16.8 us
    dot_general x1, matrix products, on_device(): jnp.einsum('necd,edf->encf', piece, w_up, preferred_element_type=jnp.floa...  16.8 us
    dot_general x1, matrix products, on_device(): jnp.einsum('necd,edf->encf', piece, w_gate, preferred_element_type=jnp.fl...  15.5 us
  transfers between devices with their start and end apart: 1, of which 1 were waited for; matrix products, arithmetic and copies ran while one was open for 0% of the time, Pallas kernels for 0%

profile of v2, /device:TPU:9, one launch (start us, length us, event | category | flops | bytes accessed | tf_op | source)
XLA Modules:
  0.0 341.8 jit_solution(7214870127926385184)
XLA Ops:
  7.6 1.5 copy.82
  11.4 21.5 %shard_map.145 = (bf16[8,768,128]{2,1,0:T(8,128)(2,1)}, bf16[2,1152,128]{2,1,0:T(8,128)(2,1)}) custom-call(bf16[2,768,128]{2,1,0:T(8,128)(2,1)} %bitcast.106, bf16[2,2,1152,128]{3,2,1,0:T(8,128)(2,1)} %bitcast.93), custom_call_target="tpu_custom_call" | custom-call | tf_op jit(solution)/shard_map/pallas_call | solution.py:141
  33.7 1.1 slice.60
  37.5 1.2 copy-done.2
  38.7 25.5 %shard_map.146 = (bf16[8,768,128]{2,1,0:T(8,128)(2,1)S(1)}, f32[8,8,768]{2,1,0:T(8,128)S(1)}) custom-call(bf16[8,768,128]{2,1,0:T(8,128)(2,1)S(1)} %copy-done.2, bf16[2304,128]{1,0:T(8,128)(2,1)S(1)} %get-tuple-element.24.k_ref, bf16[2304,256]{1,0:T(8,128)(2,1)S(1)} %concatenate.20.v_ref, s32[1,256]{1,0:T(1,128)S(1)} %bitcast.90), custom_call_target="tpu_custom_call" | custom-call | tf_op jit(solution)/shard_map/pallas_call | solution.py:255
  64.1 1.2 copy-done.3
  66.0 22.9 %shard_map.147 = (bf16[8,768,128]{2,1,0:T(8,128)(2,1)}, f32[8,8,768]{2,1,0:T(8,128)}) custom-call(bf16[8,768,128]{2,1,0:T(8,128)(2,1)} %copy-done.3, f32[8,8,768]{2,1,0:T(8,128)} %copy-done.4), custom_call_target="tpu_custom_call" | custom-call | tf_op jit(solution)/shard_map/pallas_call | solution.py:141
  90.0 2.2 fusion.11
  92.6 4.6 %fusion.42 = (bf16[1,16,256,256]{3,2,1,0:T(8,128)(2,1)}, bf16[1,16,256,256]{3,2,1,0:T(8,128)(2,1)}) fusion(bf16[2,16,256,256]{3,2,1,0:T(8,128)(2,1)} %param.19), kind=kLoop, calls=%fused_computation.83 | loop fusion | bytes 8388608 | tf_op jit(solution)/shard_map/slice | solution.py:49
  97.2 2.8 copy.107
  101.0 2.9 copy.108
  106.4 5.5 %shard_map.148 = f32[4,16,256]{2,1,0:T(8,128)} custom-call(f32[1,16,256]{2,1,0:T(8,128)} %pad_bitcast_fusion.refs_0_), custom_call_target="tpu_custom_call" | custom-call | tf_op jit(solution)/shard_map/pallas_call | solution.py:141
  113.8 1.5 convolution_convert_fusion
  115.2 25.6 %shard_map.149 = bf16[4,2,40,1536]{3,2,1,0:T(8,128)(2,1)} custom-call(bf16[4,2,40,1536]{3,2,1,0:T(8,128)(2,1)} %bitcast.109), custom_call_target="tpu_custom_call" | custom-call | tf_op jit(solution)/shard_map/pallas_call | solution.py:141
  140.8 2.3 copy.111
  143.2 40.3 %shard_map.150 = bf16[8,2,40,6144]{3,2,1,0:T(8,128)(2,1)} custom-call(bf16[2,40,6144]{2,1,0:T(8,128)(2,1)} %bitcast.99), custom_call_target="tpu_custom_call" | custom-call | tf_op jit(solution)/shard_map/pallas_call | solution.py:212
  183.5 15.5 %fusion.4 = f32[2,8,40,1024]{3,2,1,0:T(8,128)S(1)} fusion(bf16[2,6144,1024]{2,1,0:T(8,128)(2,1)} %param.27, bf16[8,2,40,6144]{3,2,1,0:T(8,128)(2,1)} %shard_map.150), kind=kOutput, calls=%fused_computation.4 | convolution fusion | flops 8053063680 | bytes 35651584 | tf_op jit(solution)/shard_map/necd,edf->encf/dot_general | solution.py:415
  198.9 16.8 %multiply_convert_fusion = bf16[2,8,40,1024]{3,2,1,0:T(8,128)(2,1)} fusion(f32[2,8,40,1024]{3,2,1,0:T(8,128)S(1)} %fusion.4, bf16[2,6144,1024]{2,1,0:T(8,128)(2,1)} %param.28, bf16[8,2,40,6144]{3,2,1,0:T(8,128)(2,1)} %shard_map.150), kind=kOutput, calls=%fused_computation.12 | convolution fusion | flops 8056995840 | bytes 36962304 | tf_op jit(solution)/shard_map/necd,edf->encf/dot_general | solution.py:416
  215.7 17.0 %fusion.6 = bf16[2,8,40,6144]{3,2,1,0:T(8,128)(2,1)S(1)} fusion(bf16[2,8,40,1024]{3,2,1,0:T(8,128)(2,1)} %multiply_convert_fusion, bf16[2,1024,6144]{2,1,0:T(8,128)(2,1)} %param.29), kind=kOutput, calls=%fused_computation.6 | convolution fusion | flops 8056995840 | bytes 34340864 | tf_op jit(solution)/shard_map/encf,efd->nced/dot_general | solution.py:418
  232.7 3.6 %copy.112 = bf16[2,40,8,6144]{3,2,0,1:T(8,128)(2,1)} copy(bf16[2,40,8,6144]{3,2,1,0:T(8,128)(2,1)S(1)} %bitcast.95) | data formatting | bytes 15728640
  236.3 68.4 %reduce-scatter.4.cloned.1.call-done = bf16[40,12288]{1,0:T(8,128)(2,1)} async-done(((bf16[320,12288]{1,0:T(8,128)(2,1)}), bf16[40,12288]{1,0:T(8,128)(2,1)}) %reduce-scatter.4.cloned.1.call-update) | async-done | bytes 983056
  304.7 1.3 copy.122
  307.1 25.0 %shard_map.151 = bf16[4,2,40,1536]{3,2,1,0:T(8,128)(2,1)} custom-call(bf16[4,2,40,1536]{3,2,1,0:T(8,128)(2,1)} %bitcast.101), custom_call_target="tpu_custom_call" | custom-call | tf_op jit(solution)/shard_map/pallas_call | solution.py:141
  332.1 2.8 fusion.12
  (99 shorter events, 15.1 us)
Async XLA Ops:
  6.5 98.6 %copy-start = (bf16[1536,8]{0,1:T(8,128)(2,1)S(1)}, bf16[1536,8]{0,1:T(8,128)(2,1)}, u32[]{:S(2)}) copy-start(bf16[1536,8]{0,1:T(8,128)(2,1)} %param.24) | copy-start | bytes 73732
  6.5 298.1 %reduce-scatter.4.cloned.1.call-start = ((), (), s32[]{:S(2)}) async-start(), calls=%async_computation.1 | async-start | bytes 8847360
  9.2 1.0 copy-start.11
  9.9 1.4 copy-start.5
  10.2 24.7 %copy-start.16 = (s32[16]{0:T(128)S(1)}, s32[16]{0:T(128)}, u32[]{:S(2)}) copy-start(s32[16]{0:T(128)} %param.21) | copy-start | bytes 196
  10.2 24.7 %copy-start.15 = (bf16[1536]{0:T(1024)(128)(2,1)S(1)}, bf16[1536]{0:T(1024)(128)(2,1)}, u32[]{:S(2)}) copy-start(bf16[1536]{0:T(1024)(128)(2,1)} %param.23) | copy-start | bytes 9220
  10.2 24.7 %copy-start.14 = (bf16[2,16,256]{2,1,0:T(8,128)(2,1)S(1)}, bf16[2,16,256]{2,1,0:T(8,128)(2,1)}, u32[]{:S(2)}) copy-start(bf16[2,16,256]{2,1,0:T(8,128)(2,1)} %param.20) | copy-start | bytes 49156
  10.2 24.8 %copy-start.12 = (bf16[16,1536]{1,0:T(8,128)(2,1)S(1)}, bf16[16,1536]{1,0:T(8,128)(2,1)}, u32[]{:S(2)}) copy-start(bf16[16,1536]{1,0:T(8,128)(2,1)} %param.18) | copy-start | bytes 147460
  10.2 24.9 %copy-start.13 = (s32[144,2]{0,1:T(2,128)S(1)}, s32[144,2]{0,1:T(2,128)}, u32[]{:S(2)}) copy-start(s32[144,2]{0,1:T(2,128)} %param.25) | copy-start | bytes 3460
  10.2 26.4 %copy-start.17 = (s32[8]{0:T(128)S(1)}, s32[8]{0:T(128)}, u32[]{:S(2)}) copy-start(s32[8]{0:T(128)} %param.26) | copy-start | bytes 100
  37.2 1.4 copy-start.2
  64.1 1.2 copy-start.3
  65.3 0.7 copy-start.4
  103.9 1.0 copy-start.6
  104.9 10.4 %copy-start.9 = (bf16[16,1536]{1,0:T(8,128)(2,1)}, bf16[16,1536]{1,0:T(8,128)(2,1)S(1)}, u32[]{:S(2)}) copy-start(bf16[16,1536]{1,0:T(8,128)(2,1)S(1)} %convert_element_type.94) | copy-start | bytes 147460
  305.9 26.2 %copy-start.7 = (bf16[144,1536]{1,0:T(8,128)(2,1)S(1)}, bf16[144,1536]{1,0:T(8,128)(2,1)}, u32[]{:S(2)}) copy-start(bf16[144,1536]{1,0:T(8,128)(2,1)} %param.22) | copy-start | bytes 1327108
  305.9 26.2 %copy-start.8 = (f32[144,320]{1,0:T(8,128)S(1)}, f32[144,320]{1,0:T(8,128)}, u32[]{:S(2)}) copy-start(f32[144,320]{1,0:T(8,128)} %get-tuple-element.18) | copy-start | bytes 552964
  306.0 26.2 %copy-start.10 = (bf16[16,1536]{1,0:T(8,128)(2,1)S(1)}, bf16[16,1536]{1,0:T(8,128)(2,1)}, u32[]{:S(2)}) copy-start(bf16[16,1536]{1,0:T(8,128)(2,1)} %copy-done.9) | copy-start | bytes 147460
  306.0 29.0 %copy-start.1 = (bf16[1536,8]{0,1:T(8,128)(2,1)S(1)}, bf16[1536,8]{0,1:T(8,128)(2,1)}, u32[]{:S(2)}) copy-start(bf16[1536,8]{0,1:T(8,128)(2,1)} %param.24) | copy-start | bytes 73732
Sparse Core Ops, SparseCore 0:
  236.4 68.1 reduce-scatter.3
